TPU v7x, 1024 devices: a whole 4x4x32 slice. The times are simulated.
1024 devices in a mesh: rep: 32 (over x, y, core), blk: 32 (over z).
Axes of the slice: x: 4, y: 4, z: 32, core: 2. Of those that a mesh axis runs over, the one named last changes fastest.
Arguments:
- grad_partial: bfloat16 [32, 512, 32, 512], P('rep', 'blk')
- owner_slot: int32 [32], replicated, may hold values from 0 to 31, each once
- left_root: bfloat16 [32, 512, 512], P('blk', 'rep')
- right_root: bfloat16 [32, 512, 512], P('blk')
- stat_left: float32 [32, 512, 512], P('blk', 'rep'), may hold values from -6 to 6
- stat_right: float32 [32, 512, 512], P('blk', 'rep'), may hold values from -6 to 6
- first_moment: float32 [32, 512, 512], P('blk', 'rep')
- second_moment: float32 [32, 512, 512], P('blk', 'rep'), may hold values from 0.5 to 20
Outputs:
- update: float32 [32, 512, 512], P('blk', 'rep')
- left_next: float32 [32, 512, 512], P('blk', 'rep')
- right_next: float32 [32, 512, 512], P('blk', 'rep')
- moment_one: float32 [32, 512, 512], P('blk', 'rep')
- moment_two: float32 [32, 512, 512], P('blk', 'rep')
Inputs may be any that keep to these rules, and one draw needn't show every extreme that they name: `owner_slot`: each slot number appears once.
All inputs are finite; a program needn't handle non-finite values.
Results may differ from a plain program's by a relative error of at most 0.0023.
The roundings to bfloat16 on the way count: a program that leaves them out, or rounds other values in their place, can miss the bound.
Values may be sent and summed in bfloat16 or wider, within the bound.
A program may use at most 32 MiB of HBM per device.

v0:
```python
import jax
import jax.numpy as jnp
from jax import lax
from jax.sharding import PartitionSpec as P


def on_device(
    grad_partial,
    owner_slot,
    left_root,
    right_root,
    stat_left,
    stat_right,
    first_moment,
    second_moment,
):
    grad_rows = grad_partial[0]
    num_blocks = owner_slot.shape[0]
    block_of = (
        jnp.zeros((num_blocks,), jnp.int32)
        .at[owner_slot]
        .set(jnp.arange(num_blocks, dtype=jnp.int32))
    )
    ordered = jnp.take(grad_rows, block_of, axis=1).astype(jnp.float32)
    summed = lax.psum_scatter(ordered, "rep", scatter_dimension=2, tiled=True).astype(jnp.bfloat16)
    flat_grad = lax.all_gather(summed, "rep", axis=2, tiled=True)
    whole_grad = lax.all_to_all(flat_grad, "blk", split_axis=1, concat_axis=0, tiled=True)
    slab_rows = stat_left.shape[1]
    first_row = lax.axis_index("rep") * slab_rows
    row_slab = lax.dynamic_slice_in_dim(whole_grad, first_row, slab_rows, 0)
    col_slab = lax.dynamic_slice_in_dim(whole_grad, first_row, slab_rows, 2)
    left_next = 0.9 * stat_left + 0.1 * jnp.einsum(
        "ikj,lkj->kil", row_slab, whole_grad, preferred_element_type=jnp.float32
    )
    right_next = 0.9 * stat_right + 0.1 * jnp.einsum(
        "ikc,ikj->kcj", col_slab, whole_grad, preferred_element_type=jnp.float32
    )
    half_step = jnp.einsum(
        "kil,lkj->kij", left_root, whole_grad, preferred_element_type=jnp.float32
    ).astype(jnp.bfloat16)
    precond = jnp.einsum("kij,kjm->kim", half_step, right_root, preferred_element_type=jnp.float32)
    grad_float = jnp.transpose(row_slab, (1, 0, 2)).astype(jnp.float32)
    moment_one = 0.9 * first_moment + 0.1 * grad_float
    moment_two = 0.95 * second_moment + 0.05 * grad_float * grad_float
    adam_dir = moment_one / (jnp.sqrt(moment_two) + 1e-08)
    adam_sum, precond_sum = lax.psum(
        (jnp.sum(adam_dir * adam_dir, axis=(1, 2)), jnp.sum(precond * precond, axis=(1, 2))), "rep"
    )
    factor = jnp.sqrt(adam_sum / (precond_sum + 1e-06))
    update = factor[:, None, None] * precond
    return (update, left_next, right_next, moment_one, moment_two)


def solution(mesh):
    in_specs = (
        P("rep", "blk", None, None),
        P(),
        P("blk", "rep", None),
        P("blk", None, None),
        P("blk", "rep", None),
        P("blk", "rep", None),
        P("blk", "rep", None),
        P("blk", "rep", None),
    )
    out_specs = (
        P("blk", "rep", None),
        P("blk", "rep", None),
        P("blk", "rep", None),
        P("blk", "rep", None),
        P("blk", "rep", None),
    )
    return jax.shard_map(
        on_device, mesh=mesh, in_specs=in_specs, out_specs=out_specs, check_vma=False
    )
```

profile of v0, /device:TPU:1, one launch (start us, length us, event | category | flops | bytes accessed | tf_op | source)
XLA Modules:
  0.0 352.4 jit_solution(12603473784507395484)
XLA Ops:
  7.2 0.0 copy-start
  7.2 0.0 reduce-scatter.2.cloned.1.call-start
  7.2 0.7 compare_select_fusion.1
  7.9 0.7 scatter_custom_fusion
  8.6 1.3 copy.19
  10.0 0.6 gather_fusion
  10.6 0.1 convert_bitcast_fusion
  10.7 3.9 %copy.16 = f32[16,32,512]{1,0,2:T(8,128)} copy(f32[16,32,512]{2,0,1:T(8,128)S(1)} %convert_bitcast_fusion) | data formatting | bytes 2097152 | tf_op jit(solution)/shard_map/convert_element_type | solution.py:24
  14.6 0.0 reduce-scatter.2.cloned.1.call-update
  14.6 0.0 copy-start.3
  14.6 0.0 copy-start.1
  14.6 0.0 copy-start.2
  14.7 142.7 %reduce-scatter.2.cloned.1.call-done = f32[16,32,16]{1,0,2:T(8,128)} async-done(((f32[16,32,512]{1,0,2:T(8,128)}), f32[16,32,16]{1,0,2:T(8,128)}) %reduce-scatter.2.cloned.1.call-update) | async-done | bytes 32784 | tf_op jit(solution)/shard_map/reduce_scatter | solution.py:25
  157.4 0.9 convert_element_type.30
  158.3 27.6 %all_gather.3 = bf16[16,32,512]{1,0,2:T(8,128)(2,1)S(1)} all-gather(bf16[16,32,16]{1,0,2:T(8,128)(2,1)S(1)} %convert_element_type.30), channel_id=1, replica_groups=mesh['rep'=32,'blk'=32] {'rep'}, dimensions={2}, use_global_device_ids=true | all-gather | bytes 540672 | tf_op jit(solution)/shard_map/all_gather | solution.py:26
  185.8 2.9 copy.17
  188.7 22.5 %all-to-all-start = ((bf16[16,32,512]{2,0,1:T(8,128)(2,1)}), bf16[16,32,512]{2,0,1:T(8,128)(2,1)S(1)}, u32[]{:S(2)}, u32[]{:S(2)}) async-start(bf16[16,32,512]{2,0,1:T(8,128)(2,1)} %copy.17), calls=%async_computation.1 | async-start | bytes 1048576 | tf_op jit(solution)/shard_map/all_to_all | solution.py:27
  211.2 64.5 %all-to-all-done = bf16[16,32,512]{2,0,1:T(8,128)(2,1)S(1)} async-done(((bf16[16,32,512]{2,0,1:T(8,128)(2,1)}), bf16[16,32,512]{2,0,1:T(8,128)(2,1)S(1)}, u32[]{:S(2)}, u32[]{:S(2)}) %all-to-all-start) | async-done | bytes 524320 | tf_op jit(solution)/shard_map/all_to_all | solution.py:27
  275.7 0.9 multiply_reduce_fusion
  276.7 1.2 multiply_reduce_fusion.1
  277.9 63.9 %all-reduce = (f32[1]{0:T(128)}, f32[1]{0:T(128)}) all-reduce(f32[1]{0:T(128)} %bitcast.7, f32[1]{0:T(128)} %bitcast.12), channel_id=1, replica_groups=mesh['rep'=32,'blk'=32] {'rep'}, use_global_device_ids=true, to_apply=%region_3.4 | all-reduce | flops 2 | bytes 16 | tf_op jit(solution)/shard_map/psum | solution.py:46
  343.1 0.9 fusion.3
  344.0 0.9 fusion.1
  344.9 0.6 multiply_bitcast_fusion
  (12 shorter events, 0.0 us)
Async XLA Ops:
  7.2 268.6 %copy-start = (bf16[1,512,512]{2,1,0:T(8,128)(2,1)S(1)}, bf16[1,512,512]{2,1,0:T(8,128)(2,1)}, u32[]{:S(2)}) copy-start(bf16[1,512,512]{2,1,0:T(8,128)(2,1)} %param.11) | copy-start | bytes 1572868
  7.2 150.2 %reduce-scatter.2.cloned.1.call-start = ((), (), s32[]{:S(2)}) async-start(), calls=%async_computation.2 | async-start | bytes 4325376 | tf_op jit(solution)/shard_map/reduce_scatter | solution.py:25
  14.6 261.1 %copy-start.5 = (bf16[1,16,512]{2,1,0:T(8,128)(2,1)S(1)}, bf16[1,16,512]{2,1,0:T(8,128)(2,1)}, u32[]{:S(2)}) copy-start(bf16[1,16,512]{2,1,0:T(8,128)(2,1)} %param.10) | copy-start | bytes 49156
  14.6 262.1 %copy-start.3 = (f32[1,16,512]{2,1,0:T(8,128)S(1)}, f32[1,16,512]{2,1,0:T(8,128)}, u32[]{:S(2)}) copy-start(f32[1,16,512]{2,1,0:T(8,128)} %param.15) | copy-start | bytes 98308
  14.6 262.1 %copy-start.4 = (f32[1,16,512]{2,1,0:T(8,128)S(1)}, f32[1,16,512]{2,1,0:T(8,128)}, u32[]{:S(2)}) copy-start(f32[1,16,512]{2,1,0:T(8,128)} %param.14) | copy-start | bytes 98308
  14.6 328.5 %copy-start.1 = (f32[1,16,512]{2,1,0:T(8,128)S(1)}, f32[1,16,512]{2,1,0:T(8,128)}, u32[]{:S(2)}) copy-start(f32[1,16,512]{2,1,0:T(8,128)} %param.12) | copy-start | bytes 98308
  14.6 329.4 %copy-start.2 = (f32[1,16,512]{2,1,0:T(8,128)S(1)}, f32[1,16,512]{2,1,0:T(8,128)}, u32[]{:S(2)}) copy-start(f32[1,16,512]{2,1,0:T(8,128)} %param.13) | copy-start | bytes 98308
  188.7 87.0 %all-to-all-start = ((bf16[16,32,512]{2,0,1:T(8,128)(2,1)}), bf16[16,32,512]{2,0,1:T(8,128)(2,1)S(1)}, u32[]{:S(2)}, u32[]{:S(2)}) async-start(bf16[16,32,512]{2,0,1:T(8,128)(2,1)} %copy.17), calls=%async_computation.1 | async-start | bytes 1048576 | tf_op jit(solution)/shard_map/all_to_all | solution.py:27
Sparse Core Ops, SparseCore 0:
  14.7 142.5 reduce-scatter.1
where the time goes:
time: 353 us; the launch traced here: 352 us
  waiting for transfers between devices  207 us (59%)
  blocking collectives  91.4 us (26%)
  starting transfers between devices  22.5 us (6%)
  between operations  15.5 us (4%)
  local copies, waits for them, and re-layouts  9.35 us (3%)
  other arithmetic  3.63 us (1%)
    reduce_scatter x1, waiting for transfers between devices, on_device(): lax.psum_scatter(ordered, 'rep', scatter_dimension=2, tiled=True)  143 us
    all_to_all x1, waiting for transfers between devices, on_device(): lax.all_to_all(flat_grad, 'blk', split_axis=1, concat_axis=0, tiled=True)  64.5 us
    psum x1, blocking collectives, on_device(): lax.psum((jnp.sum(adam_dir * adam_dir, axis=(1, 2)), jnp.sum(precond * pr...  63.9 us
    all_gather x1, blocking collectives, on_device(): flat_grad = lax.all_gather(summed, 'rep', axis=2, tiled=True)  27.6 us
    all_to_all x1, starting transfers between devices, on_device(): lax.all_to_all(flat_grad, 'blk', split_axis=1, concat_axis=0, tiled=True)  22.5 us
  transfers between devices with their start and end apart: 2, of which 2 were waited for; matrix products, arithmetic and copies ran while one was open for 0% of the time, Pallas kernels for 0%

commit v1 on v0

v1 whole, which is shorter than its diff:
```python
import jax
import jax.numpy as jnp
from jax import lax
from jax.experimental import pallas as pl
from jax.experimental.pallas import tpu as pltpu
from jax.sharding import PartitionSpec as P

MESH = pl.DeviceIdType.MESH
NX, NY, NC = 4, 4, 2
STEPS = [
    (dx, dy, dc) for dx in range(NX) for dy in range(NY) for dc in range(NC) if dx or dy or dc
]


def step_kernel(
    owner_ref,
    grad_hbm,
    lroot_hbm,
    rroot_hbm,
    sleft_hbm,
    sright_hbm,
    mone_hbm,
    mtwo_hbm,
    update_ref,
    left_ref,
    right_ref,
    one_ref,
    two_ref,
    grad_v,
    ordered,
    land,
    summed,
    gfull,
    lroot_v,
    rroot_v,
    sleft_v,
    sright_v,
    mone_v,
    mtwo_v,
    sums_v,
    sums_land,
    load_sem,
    send_sem,
    recv_sem,
):
    r = lax.axis_index("rep")
    z = lax.axis_index("blk")
    n = NX * NY * NC
    rows = summed.shape[0]
    x, y, c = r // (NY * NC), (r // NC) % NY, r % NC

    def peer_of(step):
        dx, dy, dc = step
        px, py, pc = lax.rem(x + dx, NX), lax.rem(y + dy, NY), lax.rem(c + dc, NC)
        return (px * NY + py) * NC + pc

    loads = [
        pltpu.make_async_copy(src, dst, load_sem.at[k])
        for k, (src, dst) in enumerate(
            [
                (grad_hbm, grad_v),
                (lroot_hbm, lroot_v),
                (rroot_hbm, rroot_v),
                (sleft_hbm, sleft_v),
                (sright_hbm, sright_v),
                (mone_hbm, mone_v),
                (mtwo_hbm, mtwo_v),
            ]
        )
    ]
    loads[0].start()

    barrier = pltpu.get_barrier_semaphore()
    for step in STEPS:
        pl.semaphore_signal(barrier, inc=1, device_id=(peer_of(step), z), device_id_type=MESH)

    @pl.when(r != z)
    def _():
        pl.semaphore_signal(barrier, inc=1, device_id=(z, r), device_id_type=MESH)

    for load in loads[1:]:
        load.start()

    nb = owner_ref.shape[0]
    total_rows = grad_v.shape[0]
    lane = lax.broadcasted_iota(jnp.int32, (1, total_rows), 1)
    target = jnp.zeros((1, total_rows), jnp.int32)
    for b in range(nb):
        target = jnp.where(lane % nb == b, owner_ref[b], target)
    target = target * rows + lane // nb
    loads[0].wait()
    chunk = 128
    for k in range(total_rows // chunk):
        row = lax.broadcasted_iota(jnp.int32, (chunk, total_rows), 0) + k * chunk
        pick = jnp.where(row == target, 1.0, 0.0).astype(jnp.bfloat16)
        part = jnp.dot(pick, grad_v[...], preferred_element_type=jnp.float32)
        ordered[pl.ds(k * chunk, chunk), :] = part.astype(jnp.bfloat16)

    @pl.when(r != z)
    def _():
        pl.semaphore_wait(barrier, n)

    @pl.when(r == z)
    def _():
        pl.semaphore_wait(barrier, n - 1)

    def wait_bytes(ref, sem):
        pltpu.make_async_copy(ref, ref, sem).wait()

    for k, step in enumerate(STEPS):
        peer = peer_of(step)
        pltpu.make_async_remote_copy(
            src_ref=ordered.at[pl.ds(pl.multiple_of(peer * rows, rows), rows), :],
            dst_ref=land.at[pl.ds(k * rows, rows), :],
            send_sem=send_sem.at[0],
            recv_sem=recv_sem.at[0],
            device_id=(peer, z),
            device_id_type=MESH,
        ).start()
    own = pl.ds(pl.multiple_of(r * rows, rows), rows)
    acc = ordered[own, :].astype(jnp.float32)
    wait_bytes(land, recv_sem.at[0])
    for k in range(n - 1):
        acc = acc + land[pl.ds(k * rows, rows), :].astype(jnp.float32)
    slab = acc.astype(jnp.bfloat16)

    @pl.when(r == z)
    def _():
        gfull[own, :] = slab

    @pl.when(r != z)
    def _():
        summed[...] = slab
        across = pltpu.make_async_remote_copy(
            src_ref=summed,
            dst_ref=gfull.at[pl.ds(pl.multiple_of(z * rows, rows), rows), :],
            send_sem=send_sem.at[1],
            recv_sem=recv_sem.at[1],
            device_id=(z, r),
            device_id_type=MESH,
        )
        across.start()
        pltpu.make_async_copy(summed, summed, recv_sem.at[1]).wait()

    for k, step in enumerate(STEPS):
        peer = peer_of(step)
        pltpu.make_async_remote_copy(
            src_ref=gfull.at[own, :],
            dst_ref=gfull.at[own, :],
            send_sem=send_sem.at[2],
            recv_sem=recv_sem.at[2],
            device_id=(peer, z),
            device_id_type=MESH,
        ).start()

    def fold(v):
        v = v * v
        v = sum(v[:, 128 * k : 128 * (k + 1)] for k in range(v.shape[1] // 128))
        return jnp.sum(v, axis=0, keepdims=True)

    for load in loads[1:]:
        load.wait()
    grow = gfull[own, :].astype(jnp.float32)
    one = 0.9 * mone_v[...] + 0.1 * grow
    two = 0.95 * mtwo_v[...] + 0.05 * grow * grow
    one_ref[...] = one
    two_ref[...] = two
    adam = one / (jnp.sqrt(two) + 1e-08)
    adam_part = fold(adam)

    wait_bytes(gfull.at[pl.ds(0, (n - 1) * rows), :], recv_sem.at[2])
    half = jnp.dot(lroot_v[...], gfull[...], preferred_element_type=jnp.float32)
    half = half.astype(jnp.bfloat16)
    precond = jnp.dot(half, rroot_v[...], preferred_element_type=jnp.float32)
    pre_part = fold(precond)
    line = lax.broadcasted_iota(jnp.int32, sums_v.shape, 0)
    sums_v[...] = jnp.where(line == 0, adam_part, jnp.where(line == 1, pre_part, 0.0))
    for k, step in enumerate(STEPS):
        pltpu.make_async_remote_copy(
            src_ref=sums_v,
            dst_ref=sums_land.at[k],
            send_sem=send_sem.at[3],
            recv_sem=recv_sem.at[3],
            device_id=(peer_of(step), z),
            device_id_type=MESH,
        ).start()

    nt = (((1,), (1,)), ((), ()))
    gram = lax.dot_general(gfull[own, :], gfull[...], nt, preferred_element_type=jnp.float32)
    left_ref[...] = 0.9 * sleft_v[...] + 0.1 * gram
    wide = 128
    first = r * rows
    window = pl.ds(pl.multiple_of((first // wide) * wide, wide), wide)
    at = lax.broadcasted_iota(jnp.int32, (rows, wide), 1)
    want = lax.broadcasted_iota(jnp.int32, (rows, wide), 0) + first % wide
    pick = jnp.where(at == want, 1.0, 0.0).astype(jnp.bfloat16)
    cols = lax.dot_general(pick, gfull[:, window], nt, preferred_element_type=jnp.float32)
    gram = jnp.dot(cols.astype(jnp.bfloat16), gfull[...], preferred_element_type=jnp.float32)
    right_ref[...] = 0.9 * sright_v[...] + 0.1 * gram

    wait_bytes(sums_land, recv_sem.at[3])
    sums = sums_v[...]
    for k in range(n - 1):
        sums = sums + sums_land[k]
    adam_sum = jnp.sum(sums[0:1, :], axis=1, keepdims=True)
    pre_sum = jnp.sum(sums[1:2, :], axis=1, keepdims=True)
    update_ref[...] = jnp.sqrt(adam_sum / (pre_sum + 1e-06)) * precond

    wait_bytes(land, send_sem.at[0])

    @pl.when(r != z)
    def _():
        wait_bytes(summed, send_sem.at[1])

    wait_bytes(gfull.at[pl.ds(0, (n - 1) * rows), :], send_sem.at[2])
    wait_bytes(sums_land, send_sem.at[3])


def on_device(
    grad_partial,
    owner_slot,
    left_root,
    right_root,
    stat_left,
    stat_right,
    first_moment,
    second_moment,
):
    _, rows, nb, b = grad_partial.shape
    n = NX * NY * NC
    f32, bf16 = jnp.float32, jnp.bfloat16
    anywhere = pl.BlockSpec(memory_space=pl.ANY)
    vmem = pl.BlockSpec(memory_space=pltpu.VMEM)
    outs = pl.pallas_call(
        step_kernel,
        out_shape=[jax.ShapeDtypeStruct((rows, b), f32)] * 5,
        in_specs=[pl.BlockSpec(memory_space=pltpu.SMEM)] + [anywhere] * 7,
        out_specs=[vmem] * 5,
        scratch_shapes=[
            pltpu.VMEM((rows * nb, b), bf16),
            pltpu.VMEM((rows * nb, b), bf16),
            pltpu.VMEM(((n - 1) * rows, b), bf16),
            pltpu.VMEM((rows, b), bf16),
            pltpu.VMEM((b, b), bf16),
            pltpu.VMEM((rows, b), bf16),
            pltpu.VMEM((b, b), bf16),
            pltpu.VMEM((rows, b), f32),
            pltpu.VMEM((rows, b), f32),
            pltpu.VMEM((rows, b), f32),
            pltpu.VMEM((rows, b), f32),
            pltpu.VMEM((8, 128), f32),
            pltpu.VMEM((n - 1, 8, 128), f32),
            pltpu.SemaphoreType.DMA((7,)),
            pltpu.SemaphoreType.DMA((4,)),
            pltpu.SemaphoreType.DMA((4,)),
        ],
        compiler_params=pltpu.CompilerParams(
            collective_id=0, has_side_effects=True, vmem_limit_bytes=24 * 1024 * 1024
        ),
        name="shampoo_step",
    )(
        owner_slot,
        grad_partial.reshape(rows * nb, b),
        left_root[0],
        right_root[0],
        stat_left[0],
        stat_right[0],
        first_moment[0],
        second_moment[0],
    )
    return tuple(out[None] for out in outs)


def solution(mesh):
    in_specs = (
        P("rep", "blk", None, None),
        P(),
        P("blk", "rep", None),
        P("blk", None, None),
        P("blk", "rep", None),
        P("blk", "rep", None),
        P("blk", "rep", None),
        P("blk", "rep", None),
    )
    out_specs = (P("blk", "rep", None),) * 5
    return jax.shard_map(
        on_device, mesh=mesh, in_specs=in_specs, out_specs=out_specs, check_vma=False
    )
```

time: 353 us -> 75.3 us (0.21)
  waiting for transfers between devices: 207 us -> 0 us
  blocking collectives: 91.4 us -> 0 us
  Pallas kernels: 0 us -> 64.5 us
  starting transfers between devices: 22.5 us -> 0 us
  between operations: 15.5 us -> 0.66 us
  other arithmetic: 3.63 us -> 0 us
    reduce_scatter x1 -> x0, waiting for transfers between devices: 143 us -> none  [on_device(): lax.psum_scatter(ordered, 'rep', scatter_dimension=2, tiled=True)]
    all_to_all x1 -> x0, waiting for transfers between devices: 64.5 us -> none  [on_device(): lax.all_to_all(flat_grad, 'blk', split_axis=1, concat_axis=0, tiled=True)]
    pallas_call x0 -> x1, Pallas kernels: none -> 64.5 us  [on_device(): pl.pallas_call(step_kernel, out_shape=[jax.ShapeDtypeStruct((rows, b), f3...]
    psum x1 -> x0, blocking collectives: 63.9 us -> none  [on_device(): lax.psum((jnp.sum(adam_dir * adam_dir, axis=(1, 2)), jnp.sum(precond * pr...]
    all_gather x1 -> x0, blocking collectives: 27.6 us -> none  [on_device(): flat_grad = lax.all_gather(summed, 'rep', axis=2, tiled=True)]
    all_to_all x1 -> x0, starting transfers between devices: 22.5 us -> none  [on_device(): lax.all_to_all(flat_grad, 'blk', split_axis=1, concat_axis=0, tiled=True)]
    unnamed x13 -> x21, local copies, waits for them, and re-layouts: 1.38 us -> 9.55 us
    convert_element_type x1 -> x0, local copies, waits for them, and re-layouts: 3.85 us -> none  [on_device(): ordered = jnp.take(grad_rows, block_of, axis=1).astype(jnp.float32)]
  transfers between devices with their start and end apart: 2 -> 0, of which waited for: 2 -> 0; matrix products, arithmetic and copies ran while one was open for 0% -> 0% of each run, Pallas kernels for 0% -> 0%
where the time goes in v1:
time: 75.3 us; the launch traced here: 74.7 us
  Pallas kernels  64.5 us (86%)
  local copies, waits for them, and re-layouts  9.55 us (13%)
    pallas_call x1, Pallas kernels, on_device(): pl.pallas_call(step_kernel, out_shape=[jax.ShapeDtypeStruct((rows, b), f3...  64.5 us
    unnamed x21, local copies, waits for them, and re-layouts  9.55 us

profile of v1, /device:TPU:1, one launch (start us, length us, event | category | flops | bytes accessed | tf_op | source)
XLA Modules:
  0.0 74.7 jit_solution(545361493397011812)
XLA Ops:
  0.6 0.0 copy-start.7
  0.6 0.6 copy-done.7
  1.3 0.0 copy-start
  1.3 1.0 %copy-done = bf16[1,16,32,512]{3,2,1,0:T(8,128)(2,1)S(1)} copy-done((bf16[1,16,32,512]{3,2,1,0:T(8,128)(2,1)S(1)}, bf16[1,16,32,512]{3,2,1,0:T(8,128)(2,1)}, u32[]{:S(2)}) %copy-start) | copy-done | bytes 524312
  2.3 0.0 copy-start.1
  2.3 1.0 %copy-done.1 = bf16[1,512,512]{2,1,0:T(8,128)(2,1)S(1)} copy-done((bf16[1,512,512]{2,1,0:T(8,128)(2,1)S(1)}, bf16[1,512,512]{2,1,0:T(8,128)(2,1)}, u32[]{:S(2)}) %copy-start.1) | copy-done | bytes 524312
  3.4 0.0 copy-start.2
  3.4 0.8 %copy-done.2 = f32[1,16,512]{2,1,0:T(8,128)S(1)} copy-done((f32[1,16,512]{2,1,0:T(8,128)S(1)}, f32[1,16,512]{2,1,0:T(8,128)}, u32[]{:S(2)}) %copy-start.2) | copy-done | bytes 32792
  4.1 0.0 copy-start.3
  4.1 0.8 %copy-done.3 = f32[1,16,512]{2,1,0:T(8,128)S(1)} copy-done((f32[1,16,512]{2,1,0:T(8,128)S(1)}, f32[1,16,512]{2,1,0:T(8,128)}, u32[]{:S(2)}) %copy-start.3) | copy-done | bytes 32792
  4.9 0.0 copy-start.4
  4.9 0.8 %copy-done.4 = f32[1,16,512]{2,1,0:T(8,128)S(1)} copy-done((f32[1,16,512]{2,1,0:T(8,128)S(1)}, f32[1,16,512]{2,1,0:T(8,128)}, u32[]{:S(2)}) %copy-start.4) | copy-done | bytes 32792
  5.7 0.0 copy-start.5
  5.7 0.8 %copy-done.5 = f32[1,16,512]{2,1,0:T(8,128)S(1)} copy-done((f32[1,16,512]{2,1,0:T(8,128)S(1)}, f32[1,16,512]{2,1,0:T(8,128)}, u32[]{:S(2)}) %copy-start.5) | copy-done | bytes 32792
  6.4 0.0 copy-start.6
  6.4 0.7 copy-done.6
  7.1 64.5 %shampoo_step.1 = (f32[16,512]{1,0:T(8,128)S(1)}, f32[16,512]{1,0:T(8,128)S(1)}, f32[16,512]{1,0:T(8,128)S(1)}, f32[16,512]{1,0:T(8,128)S(1)}, f32[16,512]{1,0:T(8,128)S(1)}) custom-call(s32[32]{0:T(128)S(1)} %copy-done.7, bf16[512,512]{1,0:T(8,128)(2,1)S(1)} %bitcast.12, bf16[16,512]{1,0:T(8,128)(2,1)S(1)} %bitcast.23, bf16[512,512]{1,0:T(8,128)(2,1)S(1)} %bitcast.13, ...), custom_call_target="tpu_custom_call" | custom-call | tf_op jit(solution)/shard_map/shampoo_step/pallas_call | solution.py:234
  71.6 0.6 copy.18
  72.3 0.6 copy.19
  72.9 0.6 copy.20
  73.5 0.6 copy.21
  74.1 0.6 copy.22
Async XLA Ops:
  0.6 0.7 copy-start.7
  1.3 1.0 %copy-start = (bf16[1,16,32,512]{3,2,1,0:T(8,128)(2,1)S(1)}, bf16[1,16,32,512]{3,2,1,0:T(8,128)(2,1)}, u32[]{:S(2)}) copy-start(bf16[1,16,32,512]{3,2,1,0:T(8,128)(2,1)} %param.8) | copy-start | bytes 1572868
  2.3 1.0 %copy-start.1 = (bf16[1,512,512]{2,1,0:T(8,128)(2,1)S(1)}, bf16[1,512,512]{2,1,0:T(8,128)(2,1)}, u32[]{:S(2)}) copy-start(bf16[1,512,512]{2,1,0:T(8,128)(2,1)} %param.11) | copy-start | bytes 1572868
  3.4 0.8 %copy-start.2 = (f32[1,16,512]{2,1,0:T(8,128)S(1)}, f32[1,16,512]{2,1,0:T(8,128)}, u32[]{:S(2)}) copy-start(f32[1,16,512]{2,1,0:T(8,128)} %param.12) | copy-start | bytes 98308
  4.1 0.8 %copy-start.3 = (f32[1,16,512]{2,1,0:T(8,128)S(1)}, f32[1,16,512]{2,1,0:T(8,128)}, u32[]{:S(2)}) copy-start(f32[1,16,512]{2,1,0:T(8,128)} %param.13) | copy-start | bytes 98308
  4.9 0.8 %copy-start.4 = (f32[1,16,512]{2,1,0:T(8,128)S(1)}, f32[1,16,512]{2,1,0:T(8,128)}, u32[]{:S(2)}) copy-start(f32[1,16,512]{2,1,0:T(8,128)} %param.14) | copy-start | bytes 98308
  5.7 0.8 %copy-start.5 = (f32[1,16,512]{2,1,0:T(8,128)S(1)}, f32[1,16,512]{2,1,0:T(8,128)}, u32[]{:S(2)}) copy-start(f32[1,16,512]{2,1,0:T(8,128)} %param.15) | copy-start | bytes 98308
  6.4 0.7 copy-start.6

commit v2 on v1

v2 whole, which is shorter than its diff:
```python
import jax
import jax.numpy as jnp
from jax import lax
from jax.experimental import pallas as pl
from jax.experimental.pallas import tpu as pltpu
from jax.sharding import PartitionSpec as P

MESH = pl.DeviceIdType.MESH
NX, NY, NC, NZ = 4, 4, 2, 32
N = NX * NY * NC
NT = (((1,), (1,)), ((), ()))


def chip_distance(step):
    return min(step[0], NX - step[0]) + min(step[1], NY - step[1])


CHIPS = [(dx, dy) for dx in range(NX) for dy in range(NY)]
PEERS = sorted(
    [(dx, dy, dc) for dx, dy in CHIPS for dc in range(NC) if dx or dy or dc],
    key=chip_distance,
    reverse=True,
)


def rep_of(shift):
    high = shift // 16
    rank = high * (2 * (shift - 16)) + (1 - high) * (2 * (15 - shift) + 1)
    tier, k = rank // 8, rank % 8
    core, odd = tier // 2, tier % 2
    j = k + core * (1 - 2 * (k % 2))
    x = j // 2
    y = 2 * (j % 2) + (odd + x) % 2
    return (x * NY + y) * NC + core


def shift_of(rep):
    x, y, core = rep // (NY * NC), (rep // NC) % NY, rep % NC
    j = x * 2 + y // 2
    rank = (2 * core + (x + y) % 2) * 8 + j + core * (1 - 2 * (j % 2))
    odd = rank % 2
    return (1 - odd) * (16 + rank // 2) + odd * (15 - rank // 2)


def step_kernel(
    owner_hbm,
    grad_hbm,
    lroot_hbm,
    rroot_hbm,
    sleft_hbm,
    sright_hbm,
    mone_hbm,
    mtwo_hbm,
    update_ref,
    left_ref,
    right_ref,
    one_ref,
    two_ref,
    owner_s,
    grad_v,
    ordered,
    land,
    summed,
    gfull,
    lfull,
    rroot_v,
    sleft_v,
    sright_v,
    moments_v,
    moments_land,
    pre_v,
    sums_v,
    sums_land,
    load_sem,
    send_sem,
    recv_sem,
    plane_sem,
    far_sem,
):
    r = lax.axis_index("rep")
    z = lax.axis_index("blk")
    rows = summed.shape[0]
    x, y, c = r // (NY * NC), (r // NC) % NY, r % NC
    shift = shift_of(r)
    up = (z + shift) % NZ
    down = (z + NZ - shift) % NZ
    sibling = r + 1 - 2 * c

    def peer_of(step):
        dx, dy, dc = step
        return (((x + dx) % NX) * NY + (y + dy) % NY) * NC + (c + dc) % NC

    def slab_of(index):
        return pl.ds(pl.multiple_of(index * rows, rows), rows)

    def remote(src, dst, k, rep, blk):
        return pltpu.make_async_remote_copy(
            src_ref=src,
            dst_ref=dst,
            send_sem=send_sem.at[k],
            recv_sem=recv_sem.at[k],
            device_id=(rep, blk),
            device_id_type=MESH,
        )

    def wait_bytes(ref, sem):
        pltpu.make_async_copy(ref, ref, sem).wait()

    own = slab_of(r)
    pairs = [
        (grad_hbm, grad_v),
        (owner_hbm, owner_s),
        (lroot_hbm, lfull.at[own, :]),
        (mone_hbm, moments_v.at[0]),
        (mtwo_hbm, moments_v.at[1]),
        (rroot_hbm, rroot_v),
        (sleft_hbm, sleft_v),
        (sright_hbm, sright_v),
    ]
    loads = [pltpu.make_async_copy(src, dst, load_sem.at[k]) for k, (src, dst) in enumerate(pairs)]
    loads[0].start()
    loads[1].start()

    barrier = pltpu.get_barrier_semaphore()
    for dx, dy in CHIPS:
        chip = peer_of((dx, dy, 0)) - c

        @pl.when(chip != r)
        def _():
            pl.semaphore_signal(barrier, inc=1, device_id=(chip, z), device_id_type=MESH)

    @pl.when(shift != 0)
    def _():
        pl.semaphore_signal(barrier, inc=1, device_id=(r - c + 1, down), device_id_type=MESH)

    for load in loads[2:]:
        load.start()

    total_rows = grad_v.shape[0]
    nb = total_rows // rows
    lane = lax.broadcasted_iota(jnp.int32, (1, total_rows), 1)
    loads[1].wait()
    target = jnp.zeros((1, total_rows), jnp.int32)
    for b in range(nb):
        target = jnp.where(lane % nb == b, owner_s[b], target)
    target = rep_of((target + (NZ - z)) % NZ) * rows + lane // nb
    loads[0].wait()
    chunk = 128
    for k in range(total_rows // chunk):
        row = lax.broadcasted_iota(jnp.int32, (chunk, total_rows), 0) + k * chunk
        pick = jnp.where(row == target, 1.0, 0.0).astype(jnp.bfloat16)
        part = jnp.dot(pick, grad_v[...], preferred_element_type=jnp.float32)
        ordered[pl.ds(k * chunk, chunk), :] = part.astype(jnp.bfloat16)

    @pl.when(c == 0)
    def _():
        pl.semaphore_wait(barrier, N - 1)
        pl.semaphore_signal(plane_sem, inc=1, device_id=(sibling, z), device_id_type=MESH)

    @pl.when(c == 1)
    def _():
        pl.semaphore_wait(plane_sem, 1)

    for tier in range(4):
        core, odd = tier // 2, tier % 2
        for dx in (2, 1, 3, 0):
            for m in (1, 0):
                px = (x + dx) % NX
                py = (y + 2 * m + (odd + px + y) % 2) % NY
                peer = (px * NY + py) * NC + core

                @pl.when(peer != r)
                def _():
                    remote(ordered.at[slab_of(peer), :], land.at[own, :], 0, peer, z).start()

    land[own, :] = ordered[own, :]

    @pl.when(c == 1)
    def _():
        mate = shift_of(sibling)

        @pl.when((shift != 0) & (mate != 0))
        def _():
            pl.semaphore_wait(barrier, 2)

        @pl.when((shift == 0) | (mate == 0))
        def _():
            pl.semaphore_wait(barrier, 1)

        pl.semaphore_signal(far_sem, inc=1, device_id=(sibling, z), device_id_type=MESH)

    @pl.when(c == 0)
    def _():
        pl.semaphore_wait(far_sem, 1)

    wait_bytes(land.at[pl.ds(0, (N - 1) * rows), :], recv_sem.at[0])
    acc = land[pl.ds(0, rows), :].astype(jnp.float32)
    for k in range(1, N):
        acc = acc + land[pl.ds(k * rows, rows), :].astype(jnp.float32)
    slab = acc.astype(jnp.bfloat16)
    came = slab_of(down)

    @pl.when(shift == 0)
    def _():
        gfull[came, :] = slab

    @pl.when(shift != 0)
    def _():
        summed[...] = slab
        remote(summed, gfull.at[slab_of(z), :], 1, r, up).start()

    loads[2].wait()
    for step in PEERS:
        remote(lfull.at[own, :], lfull.at[own, :], 2, peer_of(step), z).start()
    loads[3].wait()
    loads[4].wait()
    holder = rep_of((z + NZ - r) % NZ)

    @pl.when(holder == r)
    def _():
        moments_land[...] = moments_v[...]

    @pl.when(holder != r)
    def _():
        remote(moments_v, moments_land, 3, holder, z).start()
        wait_bytes(moments_v, recv_sem.at[3])

    @pl.when(shift != 0)
    def _():
        wait_bytes(summed, recv_sem.at[1])

    for step in PEERS:
        remote(gfull.at[came, :], gfull.at[came, :], 4, peer_of(step), z).start()

    def blend(moments, grad):
        one = 0.9 * moments[0] + 0.1 * grad
        two = 0.95 * moments[1] + 0.05 * grad * grad
        return one, two

    def fold(v):
        v = v * v
        v = sum(v[:, 128 * k : 128 * (k + 1)] for k in range(v.shape[1] // 128))
        return jnp.sum(v, axis=0, keepdims=True)

    one, two = blend(moments_land[...], gfull[came, :].astype(jnp.float32))
    adam_part = fold(one / (jnp.sqrt(two) + 1e-08))
    sums_v[...] = adam_part
    sums_land[r] = adam_part
    for step in PEERS:
        remote(sums_v, sums_land.at[r], 5, peer_of(step), z).start()

    for load in loads[5:]:
        load.wait()
    wait_bytes(lfull.at[pl.ds(0, (N - 1) * rows), :], recv_sem.at[2])
    wait_bytes(gfull.at[pl.ds(0, (N - 1) * rows), :], recv_sem.at[4])
    pre_part = jnp.zeros((1, 128), jnp.float32)
    for k in range(total_rows // chunk):
        part = pl.ds(k * chunk, chunk)
        half = jnp.dot(lfull[part, :], gfull[...], preferred_element_type=jnp.float32)
        precond = jnp.dot(
            half.astype(jnp.bfloat16), rroot_v[...], preferred_element_type=jnp.float32
        )
        pre_v[part, :] = precond
        pre_part = pre_part + fold(precond)

    gram = lax.dot_general(gfull[own, :], gfull[...], NT, preferred_element_type=jnp.float32)
    left_ref[...] = 0.9 * sleft_v[...] + 0.1 * gram
    wide = 128
    first = r * rows
    window = pl.ds(pl.multiple_of((first // wide) * wide, wide), wide)
    at = lax.broadcasted_iota(jnp.int32, (rows, wide), 1)
    want = lax.broadcasted_iota(jnp.int32, (rows, wide), 0) + first % wide
    pick = jnp.where(at == want, 1.0, 0.0).astype(jnp.bfloat16)
    cols = lax.dot_general(pick, gfull[:, window], NT, preferred_element_type=jnp.float32)
    gram = jnp.dot(cols.astype(jnp.bfloat16), gfull[...], preferred_element_type=jnp.float32)
    right_ref[...] = 0.9 * sright_v[...] + 0.1 * gram
    one, two = blend(moments_v[...], gfull[own, :].astype(jnp.float32))
    one_ref[...] = one
    two_ref[...] = two

    wait_bytes(sums_land.at[pl.ds(0, N - 1)], recv_sem.at[5])
    adam_sum = jnp.sum(jnp.sum(sums_land[...], axis=0), axis=1, keepdims=True)
    pre_sum = jnp.sum(pre_part, axis=1, keepdims=True)
    update_ref[...] = jnp.sqrt(adam_sum / (pre_sum + 1e-06)) * pre_v[own, :]

    wait_bytes(land.at[pl.ds(0, (N - 1) * rows), :], send_sem.at[0])

    @pl.when(shift != 0)
    def _():
        wait_bytes(summed, send_sem.at[1])

    wait_bytes(lfull.at[pl.ds(0, (N - 1) * rows), :], send_sem.at[2])

    @pl.when(holder != r)
    def _():
        wait_bytes(moments_v, send_sem.at[3])

    wait_bytes(gfull.at[pl.ds(0, (N - 1) * rows), :], send_sem.at[4])
    wait_bytes(sums_land.at[pl.ds(0, N - 1)], send_sem.at[5])


def store_kernel(*refs):
    half = len(refs) // 2
    for src, dst in zip(refs[:half], refs[half:]):
        dst[...] = src[...]


def on_device(
    grad_partial,
    owner_slot,
    left_root,
    right_root,
    stat_left,
    stat_right,
    first_moment,
    second_moment,
):
    _, rows, nb, b = grad_partial.shape
    f32, bf16 = jnp.float32, jnp.bfloat16
    hbm = pl.BlockSpec(memory_space=pltpu.HBM)
    vmem = pl.BlockSpec(memory_space=pltpu.VMEM)
    shapes = [jax.ShapeDtypeStruct((rows, b), f32)] * 5
    outs = pl.pallas_call(
        step_kernel,
        out_shape=shapes,
        in_specs=[hbm] * 8,
        out_specs=[vmem] * 5,
        scratch_shapes=[
            pltpu.SMEM((nb,), jnp.int32),
            pltpu.VMEM((rows * nb, b), bf16),
            pltpu.VMEM((rows * nb, b), bf16),
            pltpu.VMEM((rows * N, b), bf16),
            pltpu.VMEM((rows, b), bf16),
            pltpu.VMEM((b, b), bf16),
            pltpu.VMEM((b, b), bf16),
            pltpu.VMEM((b, b), bf16),
            pltpu.VMEM((rows, b), f32),
            pltpu.VMEM((rows, b), f32),
            pltpu.VMEM((2, rows, b), f32),
            pltpu.VMEM((2, rows, b), f32),
            pltpu.VMEM((b, b), f32),
            pltpu.VMEM((1, 128), f32),
            pltpu.VMEM((N, 1, 128), f32),
            pltpu.SemaphoreType.DMA((8,)),
            pltpu.SemaphoreType.DMA((6,)),
            pltpu.SemaphoreType.DMA((6,)),
            pltpu.SemaphoreType.REGULAR,
            pltpu.SemaphoreType.REGULAR,
        ],
        compiler_params=pltpu.CompilerParams(
            collective_id=0, has_side_effects=True, vmem_limit_bytes=32 * 1024 * 1024
        ),
        name="shampoo_step",
    )(
        *[
            pltpu.with_memory_space_constraint(v, pltpu.HBM)
            for v in (
                owner_slot,
                grad_partial.reshape(rows * nb, b),
                left_root[0],
                right_root[0],
                stat_left[0],
                stat_right[0],
                first_moment[0],
                second_moment[0],
            )
        ]
    )
    outs = pl.pallas_call(
        store_kernel,
        out_shape=shapes,
        in_specs=[vmem] * 5,
        out_specs=[vmem] * 5,
        compiler_params=pltpu.CompilerParams(vmem_limit_bytes=4 * 1024 * 1024),
        name="store_results",
    )(*outs)
    return tuple(out[None] for out in outs)


def solution(mesh):
    in_specs = (
        P("rep", "blk", None, None),
        P(),
        P("blk", "rep", None),
        P("blk", None, None),
        P("blk", "rep", None),
        P("blk", "rep", None),
        P("blk", "rep", None),
        P("blk", "rep", None),
    )
    out_specs = (P("blk", "rep", None),) * 5
    return jax.shard_map(
        on_device, mesh=mesh, in_specs=in_specs, out_specs=out_specs, check_vma=False
    )
```

time: 75.3 us -> 52.6 us (0.70)
  Pallas kernels: 64.5 us -> 51.8 us
  local copies, waits for them, and re-layouts: 9.55 us -> 0 us
    pallas_call x1 -> x2, Pallas kernels: 64.5 us -> 51.8 us  [the longest x1 51.1 us: on_device(): pl.pallas_call(step_kernel, out_shape=shapes, in_specs=[hbm] * 8, out_spe...]
    unnamed x21 -> x0, local copies, waits for them, and re-layouts: 9.55 us -> none
where the time goes in v2:
time: 52.6 us; the launch traced here: 52.4 us
  Pallas kernels  51.8 us (98%)
  between operations  0.64 us (1%)
    pallas_call x1, Pallas kernels, on_device(): pl.pallas_call(step_kernel, out_shape=shapes, in_specs=[hbm] * 8, out_spe...  51.1 us

profile of v2, /device:TPU:1, one launch (start us, length us, event | category | flops | bytes accessed | tf_op | source)
XLA Modules:
  0.0 52.4 jit_solution(16349715369958075968)
XLA Ops:
  0.6 51.1 %shampoo_step.1 = (f32[16,512]{1,0:T(8,128)S(1)}, f32[16,512]{1,0:T(8,128)S(1)}, f32[16,512]{1,0:T(8,128)S(1)}, f32[16,512]{1,0:T(8,128)S(1)}, f32[16,512]{1,0:T(8,128)S(1)}) custom-call(s32[32]{0:T(128)} %owner_hbm.1, bf16[512,512]{1,0:T(8,128)(2,1)} %bitcast.12, bf16[16,512]{1,0:T(8,128)(2,1)} %bitcast.18, bf16[512,512]{1,0:T(8,128)(2,1)} %bitcast.13, ...), custom_call_target="tpu_custom_call" | custom-call | tf_op jit(solution)/shard_map/shampoo_step/pallas_call | solution.py:323
  51.7 0.7 %store_results.1 = (f32[16,512]{1,0:T(8,128)}, f32[16,512]{1,0:T(8,128)}, f32[16,512]{1,0:T(8,128)}, f32[16,512]{1,0:T(8,128)}, f32[16,512]{1,0:T(8,128)}) custom-call(f32[16,512]{1,0:T(8,128)S(1)} %get-tuple-element.15.refs_0_, f32[16,512]{1,0:T(8,128)S(1)} %get-tuple-element.16.refs_1_, f32[16,512]{1,0:T(8,128)S(1)} %get-tuple-element.17.refs_2_, ...), custom_call_target="tpu_custom_call" | custom-call | tf_op jit(solution)/shard_map/store_results/pallas_call | solution.py:369

commit v3 on v2

--- a/solution.py
+++ b/solution.py
@@ -23,12 +23,23 @@
 )
 
 
+FAR = (0, 1, 2, 7, 4, 5, 6, 3)
+NEAR = (1, 0, 3, 2, 5, 4, 7, 6)
+
+
+def entry(table, k):
+    value = table[0] + 0 * k
+    for i in range(1, len(table)):
+        value = jnp.where(k == i, table[i], value)
+    return value
+
+
 def rep_of(shift):
     high = shift // 16
     rank = high * (2 * (shift - 16)) + (1 - high) * (2 * (15 - shift) + 1)
     tier, k = rank // 8, rank % 8
     core, odd = tier // 2, tier % 2
-    j = k + core * (1 - 2 * (k % 2))
+    j = (1 - core) * entry(FAR, k) + core * entry(NEAR, k)
     x = j // 2
     y = 2 * (j % 2) + (odd + x) % 2
     return (x * NY + y) * NC + core
@@ -37,7 +48,9 @@
 def shift_of(rep):
     x, y, core = rep // (NY * NC), (rep // NC) % NY, rep % NC
     j = x * 2 + y // 2
-    rank = (2 * core + (x + y) % 2) * 8 + j + core * (1 - 2 * (j % 2))
+    far = entry([FAR.index(i) for i in range(8)], j)
+    near = entry([NEAR.index(i) for i in range(8)], j)
+    rank = (2 * core + (x + y) % 2) * 8 + (1 - core) * far + core * near
     odd = rank % 2
     return (1 - odd) * (16 + rank // 2) + odd * (15 - rank // 2)
 
@@ -68,12 +81,14 @@
     sright_v,
     moments_v,
     moments_land,
+    half_v,
     pre_v,
     sums_v,
     sums_land,
     load_sem,
     send_sem,
     recv_sem,
+    slab_sem,
     plane_sem,
     far_sem,
 ):
@@ -122,7 +137,7 @@
     loads[1].start()
 
     barrier = pltpu.get_barrier_semaphore()
-    for dx, dy in CHIPS:
+    for dx, dy in sorted(CHIPS, key=chip_distance, reverse=True):
         chip = peer_of((dx, dy, 0)) - c
 
         @pl.when(chip != r)
@@ -163,15 +178,14 @@
 
     for tier in range(4):
         core, odd = tier // 2, tier % 2
-        for dx in (2, 1, 3, 0):
-            for m in (1, 0):
-                px = (x + dx) % NX
-                py = (y + 2 * m + (odd + px + y) % 2) % NY
-                peer = (px * NY + py) * NC + core
-
-                @pl.when(peer != r)
-                def _():
-                    remote(ordered.at[slab_of(peer), :], land.at[own, :], 0, peer, z).start()
+        for dx, m in ((2, 1), (2, 0), (1, 1), (3, 1), (0, 1), (1, 0), (3, 0), (0, 0)):
+            px = (x + dx) % NX
+            py = (y + 2 * m + (odd + px + y) % 2) % NY
+            peer = (px * NY + py) * NC + core
+
+            @pl.when(peer != r)
+            def _():
+                remote(ordered.at[slab_of(peer), :], land.at[own, :], 0, peer, z).start()
 
     land[own, :] = ordered[own, :]
 
@@ -229,8 +243,16 @@
     def _():
         wait_bytes(summed, recv_sem.at[1])
 
+    is_late = (down // 16) * (1 - (down // 8) % 2)
     for step in PEERS:
-        remote(gfull.at[came, :], gfull.at[came, :], 4, peer_of(step), z).start()
+        pltpu.make_async_remote_copy(
+            src_ref=gfull.at[came, :],
+            dst_ref=gfull.at[came, :],
+            send_sem=send_sem.at[4],
+            recv_sem=slab_sem.at[is_late],
+            device_id=(peer_of(step), z),
+            device_id_type=MESH,
+        ).start()
 
     def blend(moments, grad):
         one = 0.9 * moments[0] + 0.1 * grad
@@ -252,49 +274,66 @@
     for load in loads[5:]:
         load.wait()
     wait_bytes(lfull.at[pl.ds(0, (N - 1) * rows), :], recv_sem.at[2])
-    wait_bytes(gfull.at[pl.ds(0, (N - 1) * rows), :], recv_sem.at[4])
-    pre_part = jnp.zeros((1, 128), jnp.float32)
-    for k in range(total_rows // chunk):
-        part = pl.ds(k * chunk, chunk)
-        half = jnp.dot(lfull[part, :], gfull[...], preferred_element_type=jnp.float32)
-        precond = jnp.dot(
-            half.astype(jnp.bfloat16), rroot_v[...], preferred_element_type=jnp.float32
-        )
-        pre_v[part, :] = precond
-        pre_part = pre_part + fold(precond)
-
-    gram = lax.dot_general(gfull[own, :], gfull[...], NT, preferred_element_type=jnp.float32)
-    left_ref[...] = 0.9 * sleft_v[...] + 0.1 * gram
+
+    def wait_slabs(count, late):
+        @pl.when(is_late == late)
+        def _():
+            wait_bytes(gfull.at[pl.ds(0, (count - 1) * rows), :], slab_sem.at[late])
+
+        @pl.when(is_late != late)
+        def _():
+            wait_bytes(gfull.at[pl.ds(0, count * rows), :], slab_sem.at[late])
+
     wide = 128
     first = r * rows
     window = pl.ds(pl.multiple_of((first // wide) * wide, wide), wide)
     at = lax.broadcasted_iota(jnp.int32, (rows, wide), 1)
     want = lax.broadcasted_iota(jnp.int32, (rows, wide), 0) + first % wide
     pick = jnp.where(at == want, 1.0, 0.0).astype(jnp.bfloat16)
-    cols = lax.dot_general(pick, gfull[:, window], NT, preferred_element_type=jnp.float32)
-    gram = jnp.dot(cols.astype(jnp.bfloat16), gfull[...], preferred_element_type=jnp.float32)
-    right_ref[...] = 0.9 * sright_v[...] + 0.1 * gram
+
+    def half_part(ks):
+        return jnp.dot(lfull[:, ks], gfull[ks, :], preferred_element_type=jnp.float32)
+
+    def right_part(ks):
+        cols = lax.dot_general(pick, gfull[ks, window], NT, preferred_element_type=jnp.float32)
+        return jnp.dot(cols.astype(jnp.bfloat16), gfull[ks, :], preferred_element_type=jnp.float32)
+
+    early = (pl.ds(0, 256), pl.ds(384, 128))
+    late = pl.ds(256, 128)
+    wait_slabs(N - 8, 0)
+    pre_v[...] = half_part(early[0]) + half_part(early[1])
+    right_gram = right_part(early[0]) + right_part(early[1])
+    wait_bytes(land.at[pl.ds(0, (N - 1) * rows), :], send_sem.at[0])
+
+    @pl.when(shift != 0)
+    def _():
+        wait_bytes(summed, send_sem.at[1])
+
+    wait_bytes(lfull.at[pl.ds(0, (N - 1) * rows), :], send_sem.at[2])
+
+    @pl.when(holder != r)
+    def _():
+        wait_bytes(moments_v, send_sem.at[3])
+
+    wait_slabs(8, 1)
+    half_v[...] = (pre_v[...] + half_part(late)).astype(jnp.bfloat16)
+    pre_part = jnp.zeros((1, 128), jnp.float32)
+    for k in range(total_rows // chunk):
+        part = pl.ds(k * chunk, chunk)
+        precond = jnp.dot(half_v[part, :], rroot_v[...], preferred_element_type=jnp.float32)
+        pre_v[part, :] = precond
+        pre_part = pre_part + fold(precond)
+    gram = lax.dot_general(gfull[own, :], gfull[...], NT, preferred_element_type=jnp.float32)
+    left_ref[...] = 0.9 * sleft_v[...] + 0.1 * gram
+    right_ref[...] = 0.9 * sright_v[...] + 0.1 * (right_gram + right_part(late))
     one, two = blend(moments_v[...], gfull[own, :].astype(jnp.float32))
     one_ref[...] = one
     two_ref[...] = two
+    pre_sum = jnp.sum(pre_part, axis=1, keepdims=True)
 
     wait_bytes(sums_land.at[pl.ds(0, N - 1)], recv_sem.at[5])
     adam_sum = jnp.sum(jnp.sum(sums_land[...], axis=0), axis=1, keepdims=True)
-    pre_sum = jnp.sum(pre_part, axis=1, keepdims=True)
     update_ref[...] = jnp.sqrt(adam_sum / (pre_sum + 1e-06)) * pre_v[own, :]
-
-    wait_bytes(land.at[pl.ds(0, (N - 1) * rows), :], send_sem.at[0])
-
-    @pl.when(shift != 0)
-    def _():
-        wait_bytes(summed, send_sem.at[1])
-
-    wait_bytes(lfull.at[pl.ds(0, (N - 1) * rows), :], send_sem.at[2])
-
-    @pl.when(holder != r)
-    def _():
-        wait_bytes(moments_v, send_sem.at[3])
-
     wait_bytes(gfull.at[pl.ds(0, (N - 1) * rows), :], send_sem.at[4])
     wait_bytes(sums_land.at[pl.ds(0, N - 1)], send_sem.at[5])
 
@@ -338,12 +377,14 @@
             pltpu.VMEM((rows, b), f32),
             pltpu.VMEM((2, rows, b), f32),
             pltpu.VMEM((2, rows, b), f32),
+            pltpu.VMEM((b, b), bf16),
             pltpu.VMEM((b, b), f32),
             pltpu.VMEM((1, 128), f32),
             pltpu.VMEM((N, 1, 128), f32),
             pltpu.SemaphoreType.DMA((8,)),
             pltpu.SemaphoreType.DMA((6,)),
             pltpu.SemaphoreType.DMA((6,)),
+            pltpu.SemaphoreType.DMA((2,)),
             pltpu.SemaphoreType.REGULAR,
             pltpu.SemaphoreType.REGULAR,
         ],

time: 52.6 us -> 50.6 us (0.962)
  Pallas kernels: 51.8 us -> 49.8 us
    pallas_call x1, Pallas kernels: 51.1 us -> 49.1 us  [on_device(): pl.pallas_call(step_kernel, out_shape=shapes, in_specs=[hbm] * 8, out_spe...]
where the time goes in v3:
time: 50.6 us; the launch traced here: 50.4 us
  Pallas kernels  49.8 us (98%)
  between operations  0.64 us (1%)
    pallas_call x1, Pallas kernels, on_device(): pl.pallas_call(step_kernel, out_shape=shapes, in_specs=[hbm] * 8, out_spe...  49.1 us

profile of v3, /device:TPU:1, one launch (start us, length us, event | category | flops | bytes accessed | tf_op | source)
XLA Modules:
  0.0 50.4 jit_solution(13771577842709234522)
XLA Ops:
  0.6 49.1 %shampoo_step.1 = (f32[16,512]{1,0:T(8,128)S(1)}, f32[16,512]{1,0:T(8,128)S(1)}, f32[16,512]{1,0:T(8,128)S(1)}, f32[16,512]{1,0:T(8,128)S(1)}, f32[16,512]{1,0:T(8,128)S(1)}) custom-call(s32[32]{0:T(128)} %owner_hbm.1, bf16[512,512]{1,0:T(8,128)(2,1)} %bitcast.12, bf16[16,512]{1,0:T(8,128)(2,1)} %bitcast.18, bf16[512,512]{1,0:T(8,128)(2,1)} %bitcast.13, ...), custom_call_target="tpu_custom_call" | custom-call | tf_op jit(solution)/shard_map/shampoo_step/pallas_call | solution.py:362
  49.8 0.7 %store_results.1 = (f32[16,512]{1,0:T(8,128)}, f32[16,512]{1,0:T(8,128)}, f32[16,512]{1,0:T(8,128)}, f32[16,512]{1,0:T(8,128)}, f32[16,512]{1,0:T(8,128)}) custom-call(f32[16,512]{1,0:T(8,128)S(1)} %get-tuple-element.15.refs_0_, f32[16,512]{1,0:T(8,128)S(1)} %get-tuple-element.16.refs_1_, f32[16,512]{1,0:T(8,128)S(1)} %get-tuple-element.17.refs_2_, ...), custom_call_target="tpu_custom_call" | custom-call | tf_op jit(solution)/shard_map/store_results/pallas_call | solution.py:410

commit v4 on v3

--- a/solution.py
+++ b/solution.py
@@ -11,6 +11,9 @@
 NT = (((1,), (1,)), ((), ()))
 
 
+HALF = N // NC
+
+
 def chip_distance(step):
     return min(step[0], NX - step[0]) + min(step[1], NY - step[1])
 
@@ -23,6 +26,8 @@
 )
 
 
+SAME = [(dx, dy) for dx, dy, dc in PEERS if dc == 0]
+
 FAR = (0, 1, 2, 7, 4, 5, 6, 3)
 NEAR = (1, 0, 3, 2, 5, 4, 7, 6)
 
@@ -38,8 +43,9 @@
     high = shift // 16
     rank = high * (2 * (shift - 16)) + (1 - high) * (2 * (15 - shift) + 1)
     tier, k = rank // 8, rank % 8
-    core, odd = tier // 2, tier % 2
-    j = (1 - core) * entry(FAR, k) + core * entry(NEAR, k)
+    near, odd = tier // 2, tier % 2
+    core = 1 - near
+    j = core * entry(FAR, k) + near * entry(NEAR, k)
     x = j // 2
     y = 2 * (j % 2) + (odd + x) % 2
     return (x * NY + y) * NC + core
@@ -50,9 +56,13 @@
     j = x * 2 + y // 2
     far = entry([FAR.index(i) for i in range(8)], j)
     near = entry([NEAR.index(i) for i in range(8)], j)
-    rank = (2 * core + (x + y) % 2) * 8 + (1 - core) * far + core * near
+    rank = (2 * (1 - core) + (x + y) % 2) * 8 + core * far + (1 - core) * near
     odd = rank % 2
     return (1 - odd) * (16 + rank // 2) + odd * (15 - rank // 2)
+
+
+def shift_at(k, near):
+    return 16 + k // 2 + 8 * near if k % 2 == 0 else 15 - k // 2 - 8 * near
 
 
 def step_kernel(
@@ -89,6 +99,7 @@
     send_sem,
     recv_sem,
     slab_sem,
+    hand_sem,
     plane_sem,
     far_sem,
 ):
@@ -177,7 +188,7 @@
         pl.semaphore_wait(plane_sem, 1)
 
     for tier in range(4):
-        core, odd = tier // 2, tier % 2
+        core, odd = 1 - tier // 2, tier % 2
         for dx, m in ((2, 1), (2, 0), (1, 1), (3, 1), (0, 1), (1, 0), (3, 0), (0, 0)):
             px = (x + dx) % NX
             py = (y + 2 * m + (odd + px + y) % 2) % NY
@@ -243,16 +254,29 @@
     def _():
         wait_bytes(summed, recv_sem.at[1])
 
-    is_late = (down // 16) * (1 - (down // 8) % 2)
-    for step in PEERS:
+    k_own = sum(jnp.where(down == (z + NZ - shift_at(k, 1 - c)) % NZ, k, 0) for k in range(HALF))
+    piece = gfull.at[came, :]
+    for dx, dy in SAME:
         pltpu.make_async_remote_copy(
-            src_ref=gfull.at[came, :],
-            dst_ref=gfull.at[came, :],
+            src_ref=piece,
+            dst_ref=piece,
             send_sem=send_sem.at[4],
-            recv_sem=slab_sem.at[is_late],
-            device_id=(peer_of(step), z),
+            recv_sem=slab_sem.at[k_own],
+            device_id=(peer_of((dx, dy, 0)), z),
             device_id_type=MESH,
         ).start()
+
+    def hand_over(piece, k):
+        pltpu.make_async_remote_copy(
+            src_ref=piece,
+            dst_ref=piece,
+            send_sem=send_sem.at[6],
+            recv_sem=hand_sem.at[k],
+            device_id=(sibling, z),
+            device_id_type=MESH,
+        ).start()
+
+    hand_over(piece, k_own)
 
     def blend(moments, grad):
         one = 0.9 * moments[0] + 0.1 * grad
@@ -275,14 +299,22 @@
         load.wait()
     wait_bytes(lfull.at[pl.ds(0, (N - 1) * rows), :], recv_sem.at[2])
 
-    def wait_slabs(count, late):
-        @pl.when(is_late == late)
-        def _():
-            wait_bytes(gfull.at[pl.ds(0, (count - 1) * rows), :], slab_sem.at[late])
-
-        @pl.when(is_late != late)
-        def _():
-            wait_bytes(gfull.at[pl.ds(0, count * rows), :], slab_sem.at[late])
+    def wait_slabs(late):
+        for k in reversed(range(HALF)):
+            plane = (z + NZ - shift_at(k, 1 - c)) % NZ
+
+            @pl.when(((plane // 8 == 2) == late) & (k_own != k))
+            def _():
+                piece = gfull.at[slab_of(plane), :]
+                wait_bytes(piece, slab_sem.at[k])
+                hand_over(piece, k)
+
+        for k in reversed(range(HALF)):
+            plane = (z + NZ - shift_at(k, c)) % NZ
+
+            @pl.when((plane // 8 == 2) == late)
+            def _():
+                wait_bytes(gfull.at[slab_of(plane), :], hand_sem.at[k])
 
     wide = 128
     first = r * rows
@@ -300,7 +332,7 @@
 
     early = (pl.ds(0, 256), pl.ds(384, 128))
     late = pl.ds(256, 128)
-    wait_slabs(N - 8, 0)
+    wait_slabs(False)
     pre_v[...] = half_part(early[0]) + half_part(early[1])
     right_gram = right_part(early[0]) + right_part(early[1])
     wait_bytes(land.at[pl.ds(0, (N - 1) * rows), :], send_sem.at[0])
@@ -315,7 +347,7 @@
     def _():
         wait_bytes(moments_v, send_sem.at[3])
 
-    wait_slabs(8, 1)
+    wait_slabs(True)
     half_v[...] = (pre_v[...] + half_part(late)).astype(jnp.bfloat16)
     pre_part = jnp.zeros((1, 128), jnp.float32)
     for k in range(total_rows // chunk):
@@ -334,7 +366,8 @@
     wait_bytes(sums_land.at[pl.ds(0, N - 1)], recv_sem.at[5])
     adam_sum = jnp.sum(jnp.sum(sums_land[...], axis=0), axis=1, keepdims=True)
     update_ref[...] = jnp.sqrt(adam_sum / (pre_sum + 1e-06)) * pre_v[own, :]
-    wait_bytes(gfull.at[pl.ds(0, (N - 1) * rows), :], send_sem.at[4])
+    wait_bytes(gfull.at[pl.ds(0, (HALF - 1) * rows), :], send_sem.at[4])
+    wait_bytes(gfull.at[pl.ds(0, HALF * rows), :], send_sem.at[6])
     wait_bytes(sums_land.at[pl.ds(0, N - 1)], send_sem.at[5])
 
 
@@ -382,9 +415,10 @@
             pltpu.VMEM((1, 128), f32),
             pltpu.VMEM((N, 1, 128), f32),
             pltpu.SemaphoreType.DMA((8,)),
+            pltpu.SemaphoreType.DMA((7,)),
             pltpu.SemaphoreType.DMA((6,)),
-            pltpu.SemaphoreType.DMA((6,)),
-            pltpu.SemaphoreType.DMA((2,)),
+            pltpu.SemaphoreType.DMA((HALF,)),
+            pltpu.SemaphoreType.DMA((HALF,)),
             pltpu.SemaphoreType.REGULAR,
             pltpu.SemaphoreType.REGULAR,
         ],

time: 50.6 us -> 48.6 us (0.960)
  Pallas kernels: 49.8 us -> 47.8 us
    pallas_call x1, Pallas kernels: 49.1 us -> 47.2 us  [on_device(): pl.pallas_call(step_kernel, out_shape=shapes, in_specs=[hbm] * 8, out_spe...]
where the time goes in v4:
time: 48.6 us; the launch traced here: 48.5 us
  Pallas kernels  47.8 us (98%)
  between operations  0.64 us (1%)
    pallas_call x1, Pallas kernels, on_device(): pl.pallas_call(step_kernel, out_shape=shapes, in_specs=[hbm] * 8, out_spe...  47.2 us

profile of v4, /device:TPU:1, one launch (start us, length us, event | category | flops | bytes accessed | tf_op | source)
XLA Modules:
  0.0 48.5 jit_solution(17390500163251532535)
XLA Ops:
  0.6 47.2 %shampoo_step.1 = (f32[16,512]{1,0:T(8,128)S(1)}, f32[16,512]{1,0:T(8,128)S(1)}, f32[16,512]{1,0:T(8,128)S(1)}, f32[16,512]{1,0:T(8,128)S(1)}, f32[16,512]{1,0:T(8,128)S(1)}) custom-call(s32[32]{0:T(128)} %owner_hbm.1, bf16[512,512]{1,0:T(8,128)(2,1)} %bitcast.12, bf16[16,512]{1,0:T(8,128)(2,1)} %bitcast.18, bf16[512,512]{1,0:T(8,128)(2,1)} %bitcast.13, ...), custom_call_target="tpu_custom_call" | custom-call | tf_op jit(solution)/shard_map/shampoo_step/pallas_call | solution.py:395
  47.8 0.7 %store_results.1 = (f32[16,512]{1,0:T(8,128)}, f32[16,512]{1,0:T(8,128)}, f32[16,512]{1,0:T(8,128)}, f32[16,512]{1,0:T(8,128)}, f32[16,512]{1,0:T(8,128)}) custom-call(f32[16,512]{1,0:T(8,128)S(1)} %get-tuple-element.15.refs_0_, f32[16,512]{1,0:T(8,128)S(1)} %get-tuple-element.16.refs_1_, f32[16,512]{1,0:T(8,128)S(1)} %get-tuple-element.17.refs_2_, ...), custom_call_target="tpu_custom_call" | custom-call | tf_op jit(solution)/shard_map/store_results/pallas_call | solution.py:444

commit v5 on v4

--- a/solution.py
+++ b/solution.py
@@ -28,7 +28,7 @@
 
 SAME = [(dx, dy) for dx, dy, dc in PEERS if dc == 0]
 
-FAR = (0, 1, 2, 7, 4, 5, 6, 3)
+FAR = (0, 1, 2, 7, 4, 5, 3, 6)
 NEAR = (1, 0, 3, 2, 5, 4, 7, 6)
 
 

time: 48.6 us -> 47.7 us (0.981)
  Pallas kernels: 47.8 us -> 46.9 us
    pallas_call x1, Pallas kernels: 47.2 us -> 46.3 us  [on_device(): pl.pallas_call(step_kernel, out_shape=shapes, in_specs=[hbm] * 8, out_spe...]
where the time goes in v5:
time: 47.7 us; the launch traced here: 47.6 us
  Pallas kernels  46.9 us (98%)
  between operations  0.64 us (1%)
    pallas_call x1, Pallas kernels, on_device(): pl.pallas_call(step_kernel, out_shape=shapes, in_specs=[hbm] * 8, out_spe...  46.3 us

profile of v5, /device:TPU:1, one launch (start us, length us, event | category | flops | bytes accessed | tf_op | source)
XLA Modules:
  0.0 47.6 jit_solution(494535027266876493)
XLA Ops:
  0.6 46.3 %shampoo_step.1 = (f32[16,512]{1,0:T(8,128)S(1)}, f32[16,512]{1,0:T(8,128)S(1)}, f32[16,512]{1,0:T(8,128)S(1)}, f32[16,512]{1,0:T(8,128)S(1)}, f32[16,512]{1,0:T(8,128)S(1)}) custom-call(s32[32]{0:T(128)} %owner_hbm.1, bf16[512,512]{1,0:T(8,128)(2,1)} %bitcast.12, bf16[16,512]{1,0:T(8,128)(2,1)} %bitcast.18, bf16[512,512]{1,0:T(8,128)(2,1)} %bitcast.13, ...), custom_call_target="tpu_custom_call" | custom-call | tf_op jit(solution)/shard_map/shampoo_step/pallas_call | solution.py:395
  46.9 0.7 %store_results.1 = (f32[16,512]{1,0:T(8,128)}, f32[16,512]{1,0:T(8,128)}, f32[16,512]{1,0:T(8,128)}, f32[16,512]{1,0:T(8,128)}, f32[16,512]{1,0:T(8,128)}) custom-call(f32[16,512]{1,0:T(8,128)S(1)} %get-tuple-element.15.refs_0_, f32[16,512]{1,0:T(8,128)S(1)} %get-tuple-element.16.refs_1_, f32[16,512]{1,0:T(8,128)S(1)} %get-tuple-element.17.refs_2_, ...), custom_call_target="tpu_custom_call" | custom-call | tf_op jit(solution)/shard_map/store_results/pallas_call | solution.py:444

commit v6 on v5

--- a/solution.py
+++ b/solution.py
@@ -1,3 +1,5 @@
+import functools
+
 import jax
 import jax.numpy as jnp
 from jax import lax
@@ -114,7 +116,7 @@
 
     def peer_of(step):
         dx, dy, dc = step
-        return (((x + dx) % NX) * NY + (y + dy) % NY) * NC + (c + dc) % NC
+        return (lax.rem(x + dx, NX) * NY + lax.rem(y + dy, NY)) * NC + lax.rem(c + dc, NC)
 
     def slab_of(index):
         return pl.ds(pl.multiple_of(index * rows, rows), rows)
@@ -150,10 +152,12 @@
     barrier = pltpu.get_barrier_semaphore()
     for dx, dy in sorted(CHIPS, key=chip_distance, reverse=True):
         chip = peer_of((dx, dy, 0)) - c
-
-        @pl.when(chip != r)
-        def _():
+        if dx or dy:
             pl.semaphore_signal(barrier, inc=1, device_id=(chip, z), device_id_type=MESH)
+
+    @pl.when(c == 1)
+    def _():
+        pl.semaphore_signal(barrier, inc=1, device_id=(sibling, z), device_id_type=MESH)
 
     @pl.when(shift != 0)
     def _():
@@ -178,25 +182,46 @@
         part = jnp.dot(pick, grad_v[...], preferred_element_type=jnp.float32)
         ordered[pl.ds(k * chunk, chunk), :] = part.astype(jnp.bfloat16)
 
-    @pl.when(c == 0)
-    def _():
-        pl.semaphore_wait(barrier, N - 1)
-        pl.semaphore_signal(plane_sem, inc=1, device_id=(sibling, z), device_id_type=MESH)
-
-    @pl.when(c == 1)
-    def _():
-        pl.semaphore_wait(plane_sem, 1)
-
+    targets = []
     for tier in range(4):
         core, odd = 1 - tier // 2, tier % 2
         for dx, m in ((2, 1), (2, 0), (1, 1), (3, 1), (0, 1), (1, 0), (3, 0), (0, 0)):
-            px = (x + dx) % NX
-            py = (y + 2 * m + (odd + px + y) % 2) % NY
-            peer = (px * NY + py) * NC + core
-
-            @pl.when(peer != r)
-            def _():
-                remote(ordered.at[slab_of(peer), :], land.at[own, :], 0, peer, z).start()
+            px = lax.rem(x + dx, NX)
+            py = lax.rem(y + 2 * m + lax.rem(odd + px + y, 2), NY)
+            targets.append((px * NY + py) * NC + core)
+    peers = [peer_of(step) for step in PEERS]
+    same = [peer_of((dx, dy, 0)) for dx, dy in SAME]
+
+    first_hand = [lax.rem(z + NZ - shift_at(k, 1 - c), NZ) for k in range(HALF)]
+    second_hand = [lax.rem(z + NZ - shift_at(k, c), NZ) for k in range(HALF)]
+    k_own = sum(jnp.where(down == first_hand[k], k, 0) for k in range(HALF))
+
+    @pl.when(c == 0)
+    def _():
+        pl.semaphore_wait(barrier, N - 1)
+        pl.semaphore_signal(plane_sem, inc=1, device_id=(sibling, z), device_id_type=MESH)
+
+    @pl.when(c == 1)
+    def _():
+        pl.semaphore_wait(plane_sem, 1)
+
+    def scatter_to(peer):
+        remote(ordered.at[slab_of(peer), :], land.at[own, :], 0, peer, z).start()
+
+    def is_above(peer):
+        j = 2 * lax.div(peer, NY * NC) + lax.rem(lax.div(peer, 2 * NC), 2)
+        return (j < 2) | (j > 4)
+
+    above = [is_above(peer) for peer in targets[:8]]
+    for peer, up_first in zip(targets[:8], above):
+        pl.when((peer != r) & up_first)(functools.partial(scatter_to, peer))
+    for peer, up_first in zip(targets[:8], above):
+        pl.when((peer != r) & jnp.logical_not(up_first))(functools.partial(scatter_to, peer))
+    for i, peer in enumerate(targets[8:]):
+        if i % 8 < 7:
+            scatter_to(peer)
+        else:
+            pl.when(peer != r)(functools.partial(scatter_to, peer))
 
     land[own, :] = ordered[own, :]
 
@@ -235,8 +260,8 @@
         remote(summed, gfull.at[slab_of(z), :], 1, r, up).start()
 
     loads[2].wait()
-    for step in PEERS:
-        remote(lfull.at[own, :], lfull.at[own, :], 2, peer_of(step), z).start()
+    for peer in peers:
+        remote(lfull.at[own, :], lfull.at[own, :], 2, peer, z).start()
     loads[3].wait()
     loads[4].wait()
     holder = rep_of((z + NZ - r) % NZ)
@@ -254,17 +279,17 @@
     def _():
         wait_bytes(summed, recv_sem.at[1])
 
-    k_own = sum(jnp.where(down == (z + NZ - shift_at(k, 1 - c)) % NZ, k, 0) for k in range(HALF))
     piece = gfull.at[came, :]
-    for dx, dy in SAME:
-        pltpu.make_async_remote_copy(
-            src_ref=piece,
-            dst_ref=piece,
-            send_sem=send_sem.at[4],
-            recv_sem=slab_sem.at[k_own],
-            device_id=(peer_of((dx, dy, 0)), z),
-            device_id_type=MESH,
-        ).start()
+    def send_slab(reps):
+        for peer in reps:
+            pltpu.make_async_remote_copy(
+                src_ref=piece,
+                dst_ref=piece,
+                send_sem=send_sem.at[4],
+                recv_sem=slab_sem.at[k_own],
+                device_id=(peer, z),
+                device_id_type=MESH,
+            ).start()
 
     def hand_over(piece, k):
         pltpu.make_async_remote_copy(
@@ -276,8 +301,6 @@
             device_id_type=MESH,
         ).start()
 
-    hand_over(piece, k_own)
-
     def blend(moments, grad):
         one = 0.9 * moments[0] + 0.1 * grad
         two = 0.95 * moments[1] + 0.05 * grad * grad
@@ -288,12 +311,15 @@
         v = sum(v[:, 128 * k : 128 * (k + 1)] for k in range(v.shape[1] // 128))
         return jnp.sum(v, axis=0, keepdims=True)
 
+    send_slab(same[:5])
+    hand_over(piece, k_own)
     one, two = blend(moments_land[...], gfull[came, :].astype(jnp.float32))
     adam_part = fold(one / (jnp.sqrt(two) + 1e-08))
     sums_v[...] = adam_part
     sums_land[r] = adam_part
-    for step in PEERS:
-        remote(sums_v, sums_land.at[r], 5, peer_of(step), z).start()
+    for peer in peers:
+        remote(sums_v, sums_land.at[r], 5, peer, z).start()
+    send_slab(same[5:])
 
     for load in loads[5:]:
         load.wait()
@@ -301,18 +327,18 @@
 
     def wait_slabs(late):
         for k in reversed(range(HALF)):
-            plane = (z + NZ - shift_at(k, 1 - c)) % NZ
-
-            @pl.when(((plane // 8 == 2) == late) & (k_own != k))
+            plane = first_hand[k]
+
+            @pl.when(((lax.div(plane, 8) == 2) == late) & (k_own != k))
             def _():
                 piece = gfull.at[slab_of(plane), :]
                 wait_bytes(piece, slab_sem.at[k])
                 hand_over(piece, k)
 
         for k in reversed(range(HALF)):
-            plane = (z + NZ - shift_at(k, c)) % NZ
-
-            @pl.when((plane // 8 == 2) == late)
+            plane = second_hand[k]
+
+            @pl.when((lax.div(plane, 8) == 2) == late)
             def _():
                 wait_bytes(gfull.at[slab_of(plane), :], hand_sem.at[k])
 

time: 47.7 us -> 47.7 us (level)
  no operation moved by 1% of the time
where the time goes in v6:
time: 47.7 us; the launch traced here: 47.6 us
  Pallas kernels  46.9 us (98%)
  between operations  0.64 us (1%)
    pallas_call x1, Pallas kernels, on_device(): pl.pallas_call(step_kernel, out_shape=shapes, in_specs=[hbm] * 8, out_spe...  46.3 us

profile of v6, /device:TPU:1, one launch (start us, length us, event | category | flops | bytes accessed | tf_op | source)
XLA Modules:
  0.0 47.6 jit_solution(4288295880545944463)
XLA Ops:
  0.6 46.3 %shampoo_step.1 = (f32[16,512]{1,0:T(8,128)S(1)}, f32[16,512]{1,0:T(8,128)S(1)}, f32[16,512]{1,0:T(8,128)S(1)}, f32[16,512]{1,0:T(8,128)S(1)}, f32[16,512]{1,0:T(8,128)S(1)}) custom-call(s32[32]{0:T(128)} %owner_hbm.1, bf16[512,512]{1,0:T(8,128)(2,1)} %bitcast.12, bf16[16,512]{1,0:T(8,128)(2,1)} %bitcast.18, bf16[512,512]{1,0:T(8,128)(2,1)} %bitcast.13, ...), custom_call_target="tpu_custom_call" | custom-call | tf_op jit(solution)/shard_map/shampoo_step/pallas_call | solution.py:421
  46.9 0.7 %store_results.1 = (f32[16,512]{1,0:T(8,128)}, f32[16,512]{1,0:T(8,128)}, f32[16,512]{1,0:T(8,128)}, f32[16,512]{1,0:T(8,128)}, f32[16,512]{1,0:T(8,128)}) custom-call(f32[16,512]{1,0:T(8,128)S(1)} %get-tuple-element.15.refs_0_, f32[16,512]{1,0:T(8,128)S(1)} %get-tuple-element.16.refs_1_, f32[16,512]{1,0:T(8,128)S(1)} %get-tuple-element.17.refs_2_, ...), custom_call_target="tpu_custom_call" | custom-call | tf_op jit(solution)/shard_map/store_results/pallas_call | solution.py:470

commit v7 on v6

--- a/solution.py
+++ b/solution.py
@@ -30,7 +30,7 @@
 
 SAME = [(dx, dy) for dx, dy, dc in PEERS if dc == 0]
 
-FAR = (0, 1, 2, 7, 4, 5, 3, 6)
+FAR = (1, 5, 2, 7, 4, 0, 3, 6)
 NEAR = (1, 0, 3, 2, 5, 4, 7, 6)
 
 

time: 47.7 us -> 48.1 us (level)
  no operation moved by 1% of the time
where the time goes in v7:
time: 48.1 us; the launch traced here: 48 us
  Pallas kernels  47.3 us (98%)
  between operations  0.64 us (1%)
    pallas_call x1, Pallas kernels, on_device(): pl.pallas_call(step_kernel, out_shape=shapes, in_specs=[hbm] * 8, out_spe...  46.7 us

profile of v7, /device:TPU:1, one launch (start us, length us, event | category | flops | bytes accessed | tf_op | source)
XLA Modules:
  0.0 48.0 jit_solution(7310337681450361503)
XLA Ops:
  0.6 46.7 %shampoo_step.1 = (f32[16,512]{1,0:T(8,128)S(1)}, f32[16,512]{1,0:T(8,128)S(1)}, f32[16,512]{1,0:T(8,128)S(1)}, f32[16,512]{1,0:T(8,128)S(1)}, f32[16,512]{1,0:T(8,128)S(1)}) custom-call(s32[32]{0:T(128)} %owner_hbm.1, bf16[512,512]{1,0:T(8,128)(2,1)} %bitcast.12, bf16[16,512]{1,0:T(8,128)(2,1)} %bitcast.18, bf16[512,512]{1,0:T(8,128)(2,1)} %bitcast.13, ...), custom_call_target="tpu_custom_call" | custom-call | tf_op jit(solution)/shard_map/shampoo_step/pallas_call | solution.py:421
  47.3 0.7 %store_results.1 = (f32[16,512]{1,0:T(8,128)}, f32[16,512]{1,0:T(8,128)}, f32[16,512]{1,0:T(8,128)}, f32[16,512]{1,0:T(8,128)}, f32[16,512]{1,0:T(8,128)}) custom-call(f32[16,512]{1,0:T(8,128)S(1)} %get-tuple-element.15.refs_0_, f32[16,512]{1,0:T(8,128)S(1)} %get-tuple-element.16.refs_1_, f32[16,512]{1,0:T(8,128)S(1)} %get-tuple-element.17.refs_2_, ...), custom_call_target="tpu_custom_call" | custom-call | tf_op jit(solution)/shard_map/store_results/pallas_call | solution.py:470
